TPU v7x, 32 devices: a whole 2x2x4 slice. The times are simulated.
32 devices in a mesh: groups: 2 (over x), vocab: 8 (over z, y), seq: 2 (over core).
Axes of the slice: x: 2, y: 2, z: 4, core: 2. Of those that a mesh axis runs over, the one named last changes fastest.
Arguments:
- out_grad: bfloat16 [6144, 4096], P(('groups', 'vocab', 'seq')), parts along dimension 0, may hold values from -1.5 to 1.5
- token_ids: int32 [6144], P(('groups', 'vocab', 'seq')), parts along dimension 0, may hold values from 0 to 3583
- table: float32 [7168, 4096], P(('groups', 'vocab'), 'seq'), parts along dimension 0, may hold values from -6 to 6
- moment1: float32 [7168, 4096], P(('groups', 'vocab'), 'seq'), parts along dimension 0, may hold values from -1.8 to 1.8
- moment2: float32 [7168, 4096], P(('groups', 'vocab'), 'seq'), parts along dimension 0, may hold values from 0.01 to 1
Outputs:
- new_table: float32 [7168, 4096], P(('groups', 'vocab'), 'seq'), parts along dimension 0
- new_moment1: float32 [7168, 4096], P(('groups', 'vocab'), 'seq'), parts along dimension 0
- new_moment2: float32 [7168, 4096], P(('groups', 'vocab'), 'seq'), parts along dimension 0
There are 2 independent parts, one for each index of `groups`. A program takes and returns all parts, laid end to end along the dimension named above; each array names one. Nothing has to cross between parts.
All inputs are finite; a program needn't handle non-finite values.
Results may differ from a plain program's by a relative error of at most 0.00065.
Values may be sent and summed in bfloat16 or wider, within the bound.
A program may use at most 128 MiB of HBM per device.

v0:
```python
import jax
import jax.numpy as jnp
from jax import lax
from jax.sharding import PartitionSpec as P

STEP = 10


def per_device(out_grad, token_ids, table, moment1, moment2):
    slab_rows = table.shape[0]
    slab_start = lax.axis_index("vocab") * slab_rows
    slab_ids = slab_start + lax.iota(jnp.int32, slab_rows)
    grad_rows = lax.all_gather(out_grad, "vocab", axis=0, tiled=True)
    row_ids = lax.all_gather(token_ids, "vocab", axis=0, tiled=True)
    onehot = (slab_ids[:, None] == row_ids[None, :]).astype(jnp.bfloat16)
    partial_value = jnp.dot(onehot, grad_rows, preferred_element_type=jnp.float32)
    grad = lax.psum_scatter(
        partial_value.astype(jnp.bfloat16), "seq", scatter_dimension=1, tiled=True
    ).astype(jnp.float32)
    new_moment1 = 0.9 * moment1 + 0.1 * grad
    new_moment2 = 0.999 * moment2 + 0.001 * grad * grad
    first_fix = 1.0 - 0.9**STEP
    second_fix = 1.0 - 0.999**STEP
    new_table = table - 0.001 * (new_moment1 / first_fix) / (
        jnp.sqrt(new_moment2 / second_fix) + 1e-08
    )
    return (new_table, new_moment1, new_moment2)


def solution(mesh):
    placed = (
        P(("groups", "vocab", "seq"), None),
        P(("groups", "vocab", "seq")),
        P(("groups", "vocab"), "seq"),
        P(("groups", "vocab"), "seq"),
        P(("groups", "vocab"), "seq"),
    )
    return jax.shard_map(
        per_device,
        mesh=mesh,
        in_specs=placed,
        out_specs=(
            P(("groups", "vocab"), "seq"),
            P(("groups", "vocab"), "seq"),
            P(("groups", "vocab"), "seq"),
        ),
        check_vma=False,
    )
```

profile of v0, /device:TPU:0, one launch (start us, length us, event | category | flops | bytes accessed | tf_op | source)
XLA Modules:
  0.0 226.8 jit_solution(12631951196511029293)
XLA Ops:
  7.2 0.0 all-gather.2.cloned.1.call-start
  7.2 0.7 all-gather.2.cloned.1.call-update
  7.9 0.0 reduce-scatter.2.cloned.1.call-start
  8.0 1.2 dynamic-slice
  9.9 0.9 dynamic-update-slice
  10.8 13.2 %all-reduce = s32[1536]{0:T(1024)S(1)} all-reduce(s32[1536]{0:T(1024)S(1)} %dynamic-update-slice), channel_id=1, replica_groups=mesh['groups'=2,'vocab'=8,'seq'=2] {'vocab'}, use_global_device_ids=true, to_apply=%add | all-reduce | flops 1536 | bytes 12288
  24.0 165.4 %all-gather.2.cloned.1.call-done = bf16[1536,4096]{1,0:T(8,128)(2,1)} async-done(((bf16[192,4096]{1,0:T(8,128)(2,1)}), bf16[1536,4096]{1,0:T(8,128)(2,1)}) %all-gather.2.cloned.1.call-update) | async-done | bytes 12582928 | tf_op jit(solution)/shard_map/all_gather | solution.py:13
  189.4 11.9 %convolution_convert_fusion = bf16[448,4096]{1,0:T(8,128)(2,1)} fusion(bf16[1536,4096]{1,0:T(8,128)(2,1)} %all-gather.2.cloned.1.call-done, s32[1536]{0:T(1024)S(1)} %all-reduce, s32[448]{0:T(512)S(1)} %iota_add_fusion), kind=kOutput, calls=%fused_computation | convolution fusion | flops 5639667712 | bytes 16260864 | tf_op jit(solution)/shard_map/dot_general | solution.py:16
  201.3 0.0 reduce-scatter.2.cloned.1.call-update
  201.3 9.9 %reduce-scatter.2.cloned.1.call-done = bf16[448,2048]{1,0:T(8,128)(2,1)} async-done(((bf16[448,4096]{1,0:T(8,128)(2,1)}), bf16[448,2048]{1,0:T(8,128)(2,1)}) %reduce-scatter.2.cloned.1.call-update) | async-done | bytes 1835024 | tf_op jit(solution)/shard_map/reduce_scatter | solution.py:17
  211.2 8.8 %divide_subtract_fusion = (f32[448,2048]{1,0:T(8,128)}, f32[448,2048]{1,0:T(8,128)}, f32[448,2048]{1,0:T(8,128)}) fusion(f32[448,2048]{1,0:T(8,128)} %param.7, bf16[448,2048]{1,0:T(8,128)(2,1)} %reduce-scatter.2.cloned.1.call-done, f32[448,2048]{1,0:T(8,128)} %param.8, f32[448,2048]{1,0:T(8,128)} %param.9), kind=kLoop, calls=%fused_computation.5 | loop fusion | flops 11927552 | bytes 23855104 | tf_op jit(solution)/shard_map/sub | solution.py:24
  (2 shorter events, 0.0 us)
Async XLA Ops:
  7.2 182.2 %all-gather.2.cloned.1.call-start = ((), (), s32[]{:S(2)}) async-start(), calls=%async_computation.1 | async-start | bytes 14155776 | tf_op jit(solution)/shard_map/all_gather | solution.py:13
  7.9 203.3 %reduce-scatter.2.cloned.1.call-start = ((), (), s32[]{:S(2)}) async-start(), calls=%async_computation.2 | async-start | bytes 5505024 | tf_op jit(solution)/shard_map/reduce_scatter | solution.py:17
Sparse Core Ops, SparseCore 0:
  10.2 179.1 all-gather.1
  201.4 9.7 reduce-scatter.1
where the time goes:
time: 227 us
  waiting for transfers between devices  176 us (78%)
  between operations  14.7 us (6%)
  blocking collectives  13.2 us (6%)
  matrix products  11.9 us (5%)
  other arithmetic  8.8 us (4%)
    all_gather x1, waiting for transfers between devices, per_device(): grad_rows = lax.all_gather(out_grad, 'vocab', axis=0, tiled=True)  165 us
    unnamed x1, blocking collectives  13.2 us
    dot_general x1, matrix products, per_device(): jnp.dot(onehot, grad_rows, preferred_element_type=jnp.float32)  11.9 us
    reduce_scatter x1, waiting for transfers between devices, per_device(): lax.psum_scatter(partial_value.astype(jnp.bfloat16), 'seq', scatter_dimen...  9.87 us
    sub x1, other arithmetic, per_device(): table - 0.001 * (new_moment1 / first_fix) / (jnp.sqrt(new_moment2 / secon...  8.79 us
  transfers between devices with their start and end apart: 2, of which 2 were waited for; matrix products, arithmetic and copies ran while one was open for 1% of the time, Pallas kernels for 0%

commit v1 on v0

v1 whole, which is shorter than its diff:
```python
import functools

import jax
import jax.numpy as jnp
from jax import lax
from jax.experimental import pallas as pl
from jax.experimental.pallas import tpu as pltpu
from jax.sharding import PartitionSpec as P

STEP = 10
BLOCK_ROWS = 48
LANES = 128
FIRST_FIX = 1.0 - 0.9**STEP
SECOND_FIX = 1.0 - 0.999**STEP
MESH = pl.DeviceIdType.MESH


def adam(grad, table, moment1, moment2):
    new_moment1 = 0.9 * moment1 + 0.1 * grad
    new_moment2 = 0.999 * moment2 + 0.001 * grad * grad
    new_table = table - 0.001 * (new_moment1 / FIRST_FIX) / (
        jnp.sqrt(new_moment2 / SECOND_FIX) + 1e-08
    )
    return new_table, new_moment1, new_moment2


def dense_update(out_grad, token_ids, table, moment1, moment2):
    slab_rows = table.shape[0]
    slab_ids = lax.axis_index("vocab") * slab_rows + lax.iota(jnp.int32, slab_rows)
    grad_rows = lax.all_gather(out_grad, "vocab", axis=0, tiled=True)
    row_ids = lax.all_gather(token_ids, "vocab", axis=0, tiled=True)
    onehot = (slab_ids[:, None] == row_ids[None, :]).astype(jnp.bfloat16)
    partial_value = jnp.dot(onehot, grad_rows, preferred_element_type=jnp.float32)
    grad = lax.psum_scatter(
        partial_value.astype(jnp.bfloat16), "seq", scatter_dimension=1, tiled=True
    ).astype(jnp.float32)
    return adam(grad, table, moment1, moment2)


def find_slots(ids, slabs, slab_rows):
    tokens = ids.shape[1]
    row = lax.broadcasted_iota(jnp.int32, (tokens, tokens), 0)
    lane = lax.broadcasted_iota(jnp.int32, (tokens, tokens), 1)

    def slab_of(values):
        slab = jnp.zeros_like(values)
        for k in range(1, slabs):
            slab += jnp.where(values >= float(k * slab_rows), 1.0, 0.0)
        return slab

    ids_down = jnp.sum(jnp.where(row == lane, ids, 0.0), axis=1, keepdims=True)
    same = ids_down == ids
    repeat_down = jnp.max(jnp.where(same & (lane < row), 1.0, 0.0), axis=1, keepdims=True)
    repeat = jnp.max(jnp.where(same & (row < lane), 1.0, 0.0), axis=0, keepdims=True)
    slab_down = slab_of(ids_down)
    slab_first = jnp.where((repeat == 0.0) & (ids >= 0.0), slab_of(ids), -1.0)
    first_down = (repeat_down == 0.0) & (ids_down >= 0.0)
    rank_down = jnp.sum(
        jnp.where((slab_down == slab_first) & (lane < row), 1.0, 0.0), axis=1, keepdims=True
    )
    most = jnp.max(jnp.where(first_down, rank_down + 1.0, 0.0), axis=0, keepdims=True)
    slot_down = jnp.where(
        first_down & (rank_down < float(BLOCK_ROWS)),
        slab_down * float(BLOCK_ROWS) + rank_down,
        -1.0,
    )
    slot = jnp.sum(jnp.where(same, slot_down + 1.0, 0.0), axis=0, keepdims=True) - 1.0
    return slot, slot_down, ids_down, most


def route_kernel(
    groups, slabs, slab_rows,
    ids_ref, grad_ref,
    got_ref, got_ids_ref, most_ref,
    rows_ref, other_ids_ref, send_ref, note_ref, got_note_ref, count_ref, got_count_ref,
    local_sem, pair_send, pair_recv, count_send, count_recv,
    note_send, note_recv, block_send, block_recv,
):
    tokens, width = grad_ref.shape
    half = width // 2
    padded = ids_ref.shape[1]
    slots = slabs * BLOCK_ROWS
    group, me, core = lax.axis_index("groups"), lax.axis_index("vocab"), lax.axis_index("seq")
    sibling = (group, me, 1 - core)
    twins = [(lax.rem(group + d, groups), me, core) for d in range(1, groups)]
    peers = [lax.rem(me + d, slabs) for d in range(1, slabs)]

    barrier = pltpu.get_barrier_semaphore()
    for device in [sibling] + twins + [(group, peer, core) for peer in peers]:
        pl.semaphore_signal(barrier, inc=1, device_id=device, device_id_type=MESH)
    pl.semaphore_wait(barrier, groups + slabs - 1)

    def columns(which):
        return pl.ds(pl.multiple_of(which * half, half), half)

    place = pl.ds(pl.multiple_of(core * padded, padded), tokens)
    ids_copy = pltpu.make_async_remote_copy(
        ids_ref, other_ids_ref, pair_send.at[0], pair_recv.at[0],
        device_id=sibling, device_id_type=MESH,
    )
    ids_copy.start()
    rows_copy = pltpu.make_async_remote_copy(
        grad_ref.at[:, columns(1 - core)], rows_ref.at[place], pair_send.at[1], pair_recv.at[1],
        device_id=sibling, device_id_type=MESH,
    )
    rows_copy.start()
    own_rows = pltpu.make_async_copy(grad_ref.at[:, columns(core)], rows_ref.at[place], local_sem.at[0])
    own_rows.start()
    for start in (0, padded):
        if padded > tokens:
            rows_ref[start + tokens : start + padded] = jnp.zeros(
                (padded - tokens, half), rows_ref.dtype
            )

    ids_copy.wait()
    mine, other = ids_ref[0:1, :], other_ids_ref[0:1, :]
    ids = jnp.concatenate(
        [jnp.where(core == 0, mine, other), jnp.where(core == 0, other, mine)], axis=1
    ).astype(jnp.float32)
    slot, slot_down, ids_down, most = find_slots(ids, slabs, slab_rows)

    count_ref[...] = jnp.broadcast_to(most.astype(jnp.int32), count_ref.shape)
    count_copies = []
    for d, twin in enumerate(twins):
        copy = pltpu.make_async_remote_copy(
            count_ref, got_count_ref.at[d], count_send.at[d], count_recv.at[d],
            device_id=twin, device_id_type=MESH,
        )
        copy.start()
        count_copies.append(copy)

    gather = (
        lax.broadcasted_iota(jnp.int32, (slots, 2 * padded), 0) == slot.astype(jnp.int32)
    ).astype(jnp.float32).astype(jnp.bfloat16)
    own_rows.wait()
    rows_copy.wait()
    step = min(half, 512)

    @pl.loop(0, half // step)
    def _(c):
        at = pl.ds(pl.multiple_of(c * step, step), step)
        send_ref[:, at] = jnp.dot(
            gather, rows_ref[:, at], preferred_element_type=jnp.float32
        ).astype(jnp.bfloat16)

    def block(k):
        return pl.ds(pl.multiple_of(k * BLOCK_ROWS, BLOCK_ROWS), BLOCK_ROWS)

    block_copies = []
    for d, peer in enumerate(peers):
        copy = pltpu.make_async_remote_copy(
            send_ref.at[block(peer)], got_ref.at[block(me)], block_send.at[d], block_recv.at[d],
            device_id=(group, peer, core), device_id_type=MESH,
        )
        copy.start()
        block_copies.append(copy)
    own_block = pltpu.make_async_copy(
        send_ref.at[block(me)], got_ref.at[block(me)], local_sem.at[1]
    )
    own_block.start()

    for d, copy in enumerate(count_copies):
        copy.wait()
        most = jnp.maximum(most, got_count_ref[d, 0:1, 0:1].astype(jnp.float32))
    lane = lax.broadcasted_iota(jnp.int32, (2 * padded, LANES), 1)
    sub = lax.broadcasted_iota(jnp.int32, (8, LANES), 0)
    slot_down = slot_down.astype(jnp.int32)
    for k in range(slabs):
        chosen = (slot_down == lane + k * BLOCK_ROWS) & (lane < BLOCK_ROWS)
        note = jnp.sum(jnp.where(chosen, ids_down + 1.0, 0.0), axis=0, keepdims=True) - 1.0
        note_ref[k] = jnp.where(sub == 0, note, most).astype(jnp.int32)
    note_copies = []
    for d, peer in enumerate(peers):
        copy = pltpu.make_async_remote_copy(
            note_ref.at[peer], got_note_ref.at[me], note_send.at[d], note_recv.at[d],
            device_id=(group, peer, core), device_id_type=MESH,
        )
        copy.start()
        note_copies.append(copy)
    own_note = pltpu.make_async_copy(note_ref.at[me], got_note_ref.at[me], local_sem.at[2])
    own_note.start()
    own_note.wait()
    for copy in note_copies:
        copy.wait()

    row = lax.broadcasted_iota(jnp.int32, (BLOCK_ROWS, LANES), 0)
    lane = lax.broadcasted_iota(jnp.int32, (BLOCK_ROWS, LANES), 1)
    wide_row = lax.broadcasted_iota(jnp.int32, (BLOCK_ROWS, slots), 0)
    wide_lane = lax.broadcasted_iota(jnp.int32, (BLOCK_ROWS, slots), 1)
    got_ids = jnp.zeros((1, slots), jnp.float32)
    for k in range(slabs):
        note = got_note_ref[k].astype(jnp.float32)
        most = jnp.maximum(most, note[1:2, 0:1])
        down = jnp.sum(jnp.where(row == lane, note[0:1], 0.0), axis=1, keepdims=True)
        got_ids += jnp.sum(
            jnp.where(wide_lane == wide_row + k * BLOCK_ROWS, down, 0.0), axis=0, keepdims=True
        )
    got_ids_ref[...] = jnp.broadcast_to(got_ids.astype(jnp.int32), got_ids_ref.shape)
    most_ref[...] = jnp.broadcast_to(most.astype(jnp.int32), most_ref.shape)

    own_block.wait()
    for copy in block_copies:
        copy.wait()


def route(out_grad, token_ids, groups, slabs, slab_rows):
    tokens, width = out_grad.shape
    padded = -(-tokens // LANES) * LANES
    slots = slabs * BLOCK_ROWS
    half = width // 2
    ids = jnp.pad(token_ids, (0, padded - tokens), constant_values=-1)
    ids = jnp.broadcast_to(ids[None, :], (8, padded))
    vmem = pl.BlockSpec(memory_space=pltpu.VMEM)
    anywhere = pl.BlockSpec(memory_space=pl.ANY)
    dma = pltpu.SemaphoreType.DMA
    others = max(groups - 1, 1)
    return pl.pallas_call(
        functools.partial(route_kernel, groups, slabs, slab_rows),
        out_shape=(
            jax.ShapeDtypeStruct((slots, half), jnp.bfloat16),
            jax.ShapeDtypeStruct((8, slots), jnp.int32),
            jax.ShapeDtypeStruct((8, LANES), jnp.int32),
        ),
        in_specs=[vmem, anywhere],
        out_specs=(anywhere, vmem, vmem),
        scratch_shapes=[
            pltpu.VMEM((2 * padded, half), jnp.bfloat16),
            pltpu.VMEM((8, padded), jnp.int32),
            pltpu.VMEM((slots, half), jnp.bfloat16),
            pltpu.VMEM((slabs, 8, LANES), jnp.int32),
            pltpu.VMEM((slabs, 8, LANES), jnp.int32),
            pltpu.VMEM((8, LANES), jnp.int32),
            pltpu.VMEM((others, 8, LANES), jnp.int32),
            dma((3,)),
            dma((2,)),
            dma((2,)),
            dma((others,)),
            dma((others,)),
            dma((slabs - 1,)),
            dma((slabs - 1,)),
            dma((slabs - 1,)),
            dma((slabs - 1,)),
        ],
        compiler_params=pltpu.CompilerParams(
            collective_id=0, has_side_effects=True, vmem_limit_bytes=24 * 1024 * 1024
        ),
        cost_estimate=pl.CostEstimate(
            flops=4 * slots * padded * half, bytes_accessed=60_000_000, transcendentals=0
        ),
        name="route_rows",
    )(ids, out_grad)


def adam_kernel(ids_ref, got_ref, table_ref, m1_ref, m2_ref, t_out, m1_out, m2_out, onehot_ref):
    slab_rows = table_ref.shape[0]

    @pl.when(pl.program_id(0) == 0)
    def _():
        first = lax.axis_index("vocab") * slab_rows
        row = lax.broadcasted_iota(jnp.int32, onehot_ref.shape, 0) + first
        onehot_ref[...] = (
            (row == ids_ref[0:1, :]).astype(jnp.float32).astype(jnp.bfloat16)
        )

    grad = jnp.dot(onehot_ref[...], got_ref[...], preferred_element_type=jnp.float32)
    t_out[...], m1_out[...], m2_out[...] = adam(grad, table_ref[...], m1_ref[...], m2_ref[...])


def update(got, got_ids, table, moment1, moment2):
    slab_rows, half = table.shape
    slots = got.shape[0]
    step = min(half, 256)
    tile = pl.BlockSpec((slab_rows, step), lambda c: (0, c))
    shape = jax.ShapeDtypeStruct(table.shape, jnp.float32)
    return pl.pallas_call(
        adam_kernel,
        grid=(half // step,),
        out_shape=(shape,) * 3,
        in_specs=[
            pl.BlockSpec((8, slots), lambda c: (0, 0)),
            pl.BlockSpec((slots, step), lambda c: (0, c)),
            tile, tile, tile,
        ],
        out_specs=(tile,) * 3,
        scratch_shapes=[pltpu.VMEM((slab_rows, slots), jnp.bfloat16)],
        compiler_params=pltpu.CompilerParams(vmem_limit_bytes=16 * 1024 * 1024),
        cost_estimate=pl.CostEstimate(
            flops=2 * slab_rows * slots * half,
            bytes_accessed=24 * slab_rows * half,
            transcendentals=slab_rows * half,
        ),
        name="adam_update",
    )(got_ids, got, table, moment1, moment2)


def per_device(groups, slabs, out_grad, token_ids, table, moment1, moment2):
    got, got_ids, most = route(out_grad, token_ids, groups, slabs, table.shape[0])
    outs = update(got, got_ids, table, moment1, moment2)

    def again(carry):
        return (jnp.int32(0),) + dense_update(out_grad, token_ids, table, moment1, moment2)

    return lax.while_loop(lambda carry: carry[0] > BLOCK_ROWS, again, (most[0, 0],) + tuple(outs))[1:]


def solution(mesh):
    slab = P(("groups", "vocab"), "seq")
    return jax.shard_map(
        functools.partial(per_device, mesh.shape["groups"], mesh.shape["vocab"]),
        mesh=mesh,
        in_specs=(
            P(("groups", "vocab", "seq"), None), P(("groups", "vocab", "seq")), slab, slab, slab,
        ),
        out_specs=(slab, slab, slab),
        check_vma=False,
    )
```

time: 227 us -> 74.5 us (0.33)
  waiting for transfers between devices: 176 us -> 0 us
  Pallas kernels: 0 us -> 58.4 us
  blocking collectives: 13.2 us -> 0 us
  matrix products: 11.9 us -> 0 us
  other arithmetic: 8.8 us -> 0 us
    all_gather x1 -> x0, waiting for transfers between devices: 165 us -> none  [per_device(): grad_rows = lax.all_gather(out_grad, 'vocab', axis=0, tiled=True)]
    pallas_call x0 -> x2, Pallas kernels: none -> 58.4 us  [the longest x1 46.4 us: route(): pl.pallas_call(functools.partial(route_kernel, groups, slabs, slab_rows),...]
    unnamed x1 -> x0, blocking collectives: 13.2 us -> none
    dot_general x1 -> x0, matrix products: 11.9 us -> none  [per_device(): jnp.dot(onehot, grad_rows, preferred_element_type=jnp.float32)]
    reduce_scatter x1 -> x0, waiting for transfers between devices: 9.87 us -> none  [per_device(): lax.psum_scatter(partial_value.astype(jnp.bfloat16), 'seq', scatter_dimen...]
    sub x1 -> x0, other arithmetic: 8.79 us -> none  [per_device(): table - 0.001 * (new_moment1 / first_fix) / (jnp.sqrt(new_moment2 / secon...]
  transfers between devices with their start and end apart: 2 -> 0, of which waited for: 2 -> 0; matrix products, arithmetic and copies ran while one was open for 1% -> 0% of each run, Pallas kernels for 0% -> 0%
where the time goes in v1:
time: 74.5 us; the launch traced here: 74.2 us
  Pallas kernels  58.4 us (78%)
  between operations  14 us (19%)
  local copies, waits for them, and re-layouts  1.18 us (2%)
    pallas_call x1, Pallas kernels, route(): pl.pallas_call(functools.partial(route_kernel, groups, slabs, slab_rows),...  46.4 us
    pallas_call x1, Pallas kernels, update(): pl.pallas_call(adam_kernel, grid=(half // step,), out_shape=(shape,) * 3,...  12.1 us

profile of v1, /device:TPU:0, one launch (start us, length us, event | category | flops | bytes accessed | tf_op | source)
XLA Modules:
  0.0 74.2 jit_solution(1793074501067136574)
XLA Ops:
  7.2 0.7 pad.4
  7.9 46.4 %route_rows.1 = (bf16[384,2048]{1,0:T(8,128)(2,1)S(1)}, s32[8,384]{1,0:T(8,128)S(1)}, s32[8,128]{1,0:T(8,128)S(1)}) custom-call(s32[8,256]{1,0:T(8,128)S(1)} %broadcast_in_dim.2.ids_ref, bf16[192,4096]{1,0:T(8,128)(2,1)} %grad_ref.1), custom_call_target="tpu_custom_call" | custom-call | flops 805306368 | bytes 60000000 | tf_op jit(solution)/shard_map/route_rows/pallas_call | solution.py:217
  54.2 0.5 slice.3
  54.7 0.0 copy-start
  54.7 12.1 %adam_update.1 = (f32[448,2048]{1,0:T(8,128)}, f32[448,2048]{1,0:T(8,128)}, f32[448,2048]{1,0:T(8,128)}) custom-call(s32[8,384]{1,0:T(8,128)S(1)} %get-tuple-element.55.ids_ref, bf16[384,2048]{1,0:T(8,128)(2,1)S(1)} %get-tuple-element.56.got_ref, f32[448,2048]{1,0:T(8,128)} %table_ref.1, f32[448,2048]{1,0:T(8,128)} %m1_ref.1, f32[448,2048]{1,0:T(8,128)} %m2_ref.1), custom_call_target="tpu_custom_call" | custom-call | flops 704643072 | bytes 22020096 | tf_op jit(solution)/shard_map/adam_update/pallas_call | solution.py:275
  66.8 0.0 copy-done
  66.8 0.6 while.13
  (1 shorter events, 0.0 us)
Async XLA Ops:
  54.7 12.1 %copy-start = (s32[192]{0:T(256)S(1)}, s32[192]{0:T(256)}, u32[]{:S(2)}) copy-start(s32[192]{0:T(256)} %param.8) | copy-start | bytes 2308

commit v2 on v1

--- a/solution.py
+++ b/solution.py
@@ -18,8 +18,8 @@
 def adam(grad, table, moment1, moment2):
     new_moment1 = 0.9 * moment1 + 0.1 * grad
     new_moment2 = 0.999 * moment2 + 0.001 * grad * grad
-    new_table = table - 0.001 * (new_moment1 / FIRST_FIX) / (
-        jnp.sqrt(new_moment2 / SECOND_FIX) + 1e-08
+    new_table = table - new_moment1 * (0.001 / FIRST_FIX) / (
+        jnp.sqrt(new_moment2 * (1.0 / SECOND_FIX)) + 1e-08
     )
     return new_table, new_moment1, new_moment2
 
@@ -41,44 +41,47 @@
     tokens = ids.shape[1]
     row = lax.broadcasted_iota(jnp.int32, (tokens, tokens), 0)
     lane = lax.broadcasted_iota(jnp.int32, (tokens, tokens), 1)
-
-    def slab_of(values):
-        slab = jnp.zeros_like(values)
-        for k in range(1, slabs):
-            slab += jnp.where(values >= float(k * slab_rows), 1.0, 0.0)
-        return slab
-
     ids_down = jnp.sum(jnp.where(row == lane, ids, 0.0), axis=1, keepdims=True)
-    same = ids_down == ids
-    repeat_down = jnp.max(jnp.where(same & (lane < row), 1.0, 0.0), axis=1, keepdims=True)
-    repeat = jnp.max(jnp.where(same & (row < lane), 1.0, 0.0), axis=0, keepdims=True)
-    slab_down = slab_of(ids_down)
-    slab_first = jnp.where((repeat == 0.0) & (ids >= 0.0), slab_of(ids), -1.0)
-    first_down = (repeat_down == 0.0) & (ids_down >= 0.0)
-    rank_down = jnp.sum(
-        jnp.where((slab_down == slab_first) & (lane < row), 1.0, 0.0), axis=1, keepdims=True
-    )
-    most = jnp.max(jnp.where(first_down, rank_down + 1.0, 0.0), axis=0, keepdims=True)
-    slot_down = jnp.where(
-        first_down & (rank_down < float(BLOCK_ROWS)),
-        slab_down * float(BLOCK_ROWS) + rank_down,
-        -1.0,
-    )
-    slot = jnp.sum(jnp.where(same, slot_down + 1.0, 0.0), axis=0, keepdims=True) - 1.0
-    return slot, slot_down, ids_down, most
+    same = jnp.where(ids_down == ids, 1.0, 0.0)
+    before = jnp.where(row < lane, 1.0, 0.0)
+    first = 1.0 - jnp.max(same * before, axis=0, keepdims=True)
+    slab = jnp.zeros_like(ids)
+    for k in range(1, slabs):
+        slab += jnp.where(ids >= float(k * slab_rows), 1.0, 0.0)
+
+    member = jnp.where(
+        slab == lax.broadcasted_iota(jnp.int32, (slabs, tokens), 0).astype(jnp.float32), first, 0.0
+    )
+    ahead = jnp.dot(
+        member.astype(jnp.bfloat16), before.astype(jnp.bfloat16),
+        preferred_element_type=jnp.float32,
+    )
+    rank = jnp.sum(member * ahead, axis=0, keepdims=True)
+    most = jnp.max(first * (rank + 1.0), axis=1, keepdims=True)
+    fits = jnp.where(rank < float(BLOCK_ROWS), first, 0.0)
+    slot_first = fits * (slab * float(BLOCK_ROWS) + rank + 1.0) - 1.0
+
+    field = lax.broadcasted_iota(jnp.int32, (8, tokens), 0)
+    facts = jnp.where(
+        field == 0, fits * slab, jnp.where(field == 1, fits * rank, jnp.where(field == 2, fits, 0.0))
+    )
+    facts = jnp.dot(
+        facts.astype(jnp.bfloat16), same.astype(jnp.bfloat16), preferred_element_type=jnp.float32
+    )
+    slot = facts[0:1] * float(BLOCK_ROWS) + facts[1:2] + facts[2:3] - 1.0
+    return slot, slot_first, ids_down, most
 
 
 def route_kernel(
     groups, slabs, slab_rows,
-    ids_ref, grad_ref,
-    got_ref, got_ids_ref, most_ref,
+    ids_ref, grad_ref, table_ref, m1_ref, m2_ref,
+    got_ref, got_ids_ref, most_ref, near_table, near_m1, near_m2,
     rows_ref, other_ids_ref, send_ref, note_ref, got_note_ref, count_ref, got_count_ref,
-    local_sem, pair_send, pair_recv, count_send, count_recv,
+    local_sem, near_sem, pair_send, pair_recv, count_send, count_recv,
     note_send, note_recv, block_send, block_recv,
 ):
     tokens, width = grad_ref.shape
     half = width // 2
-    padded = ids_ref.shape[1]
     slots = slabs * BLOCK_ROWS
     group, me, core = lax.axis_index("groups"), lax.axis_index("vocab"), lax.axis_index("seq")
     sibling = (group, me, 1 - core)
@@ -93,7 +96,7 @@
     def columns(which):
         return pl.ds(pl.multiple_of(which * half, half), half)
 
-    place = pl.ds(pl.multiple_of(core * padded, padded), tokens)
+    place = pl.ds(pl.multiple_of(core * tokens, tokens), tokens)
     ids_copy = pltpu.make_async_remote_copy(
         ids_ref, other_ids_ref, pair_send.at[0], pair_recv.at[0],
         device_id=sibling, device_id_type=MESH,
@@ -106,18 +109,19 @@
     rows_copy.start()
     own_rows = pltpu.make_async_copy(grad_ref.at[:, columns(core)], rows_ref.at[place], local_sem.at[0])
     own_rows.start()
-    for start in (0, padded):
-        if padded > tokens:
-            rows_ref[start + tokens : start + padded] = jnp.zeros(
-                (padded - tokens, half), rows_ref.dtype
-            )
+    near = [
+        pltpu.make_async_copy(far_ref, near_ref, near_sem.at[i])
+        for i, (far_ref, near_ref) in enumerate(
+            ((table_ref, near_table), (m1_ref, near_m1), (m2_ref, near_m2))
+        )
+    ]
 
     ids_copy.wait()
-    mine, other = ids_ref[0:1, :], other_ids_ref[0:1, :]
+    mine, other = ids_ref[...], other_ids_ref[...]
     ids = jnp.concatenate(
         [jnp.where(core == 0, mine, other), jnp.where(core == 0, other, mine)], axis=1
     ).astype(jnp.float32)
-    slot, slot_down, ids_down, most = find_slots(ids, slabs, slab_rows)
+    slot, slot_first, ids_down, most = find_slots(ids, slabs, slab_rows)
 
     count_ref[...] = jnp.broadcast_to(most.astype(jnp.int32), count_ref.shape)
     count_copies = []
@@ -130,7 +134,7 @@
         count_copies.append(copy)
 
     gather = (
-        lax.broadcasted_iota(jnp.int32, (slots, 2 * padded), 0) == slot.astype(jnp.int32)
+        lax.broadcasted_iota(jnp.int32, (slots, 2 * tokens), 0) == slot.astype(jnp.int32)
     ).astype(jnp.float32).astype(jnp.bfloat16)
     own_rows.wait()
     rows_copy.wait()
@@ -158,11 +162,16 @@
         send_ref.at[block(me)], got_ref.at[block(me)], local_sem.at[1]
     )
     own_block.start()
+    for copy in near:
+        copy.start()
 
     for d, copy in enumerate(count_copies):
         copy.wait()
         most = jnp.maximum(most, got_count_ref[d, 0:1, 0:1].astype(jnp.float32))
-    lane = lax.broadcasted_iota(jnp.int32, (2 * padded, LANES), 1)
+    row = lax.broadcasted_iota(jnp.int32, (2 * tokens, 2 * tokens), 0)
+    lane = lax.broadcasted_iota(jnp.int32, (2 * tokens, 2 * tokens), 1)
+    slot_down = jnp.sum(jnp.where(row == lane, slot_first, 0.0), axis=1, keepdims=True)
+    lane = lax.broadcasted_iota(jnp.int32, (2 * tokens, LANES), 1)
     sub = lax.broadcasted_iota(jnp.int32, (8, LANES), 0)
     slot_down = slot_down.astype(jnp.int32)
     for k in range(slabs):
@@ -198,39 +207,40 @@
     got_ids_ref[...] = jnp.broadcast_to(got_ids.astype(jnp.int32), got_ids_ref.shape)
     most_ref[...] = jnp.broadcast_to(most.astype(jnp.int32), most_ref.shape)
 
+    for copy in near:
+        copy.wait()
     own_block.wait()
     for copy in block_copies:
         copy.wait()
 
 
-def route(out_grad, token_ids, groups, slabs, slab_rows):
+def route(out_grad, token_ids, table, moment1, moment2, groups, slabs):
     tokens, width = out_grad.shape
-    padded = -(-tokens // LANES) * LANES
     slots = slabs * BLOCK_ROWS
     half = width // 2
-    ids = jnp.pad(token_ids, (0, padded - tokens), constant_values=-1)
-    ids = jnp.broadcast_to(ids[None, :], (8, padded))
+    ids = token_ids.reshape(1, tokens)
     vmem = pl.BlockSpec(memory_space=pltpu.VMEM)
     anywhere = pl.BlockSpec(memory_space=pl.ANY)
     dma = pltpu.SemaphoreType.DMA
     others = max(groups - 1, 1)
     return pl.pallas_call(
-        functools.partial(route_kernel, groups, slabs, slab_rows),
+        functools.partial(route_kernel, groups, slabs, table.shape[0]),
         out_shape=(
             jax.ShapeDtypeStruct((slots, half), jnp.bfloat16),
             jax.ShapeDtypeStruct((8, slots), jnp.int32),
             jax.ShapeDtypeStruct((8, LANES), jnp.int32),
-        ),
-        in_specs=[vmem, anywhere],
-        out_specs=(anywhere, vmem, vmem),
+        ) + (jax.ShapeDtypeStruct(table.shape, jnp.float32),) * 3,
+        in_specs=[vmem] + [anywhere] * 4,
+        out_specs=(anywhere, vmem, vmem) + (anywhere,) * 3,
         scratch_shapes=[
-            pltpu.VMEM((2 * padded, half), jnp.bfloat16),
-            pltpu.VMEM((8, padded), jnp.int32),
+            pltpu.VMEM((2 * tokens, half), jnp.bfloat16),
+            pltpu.VMEM((1, tokens), jnp.int32),
             pltpu.VMEM((slots, half), jnp.bfloat16),
             pltpu.VMEM((slabs, 8, LANES), jnp.int32),
             pltpu.VMEM((slabs, 8, LANES), jnp.int32),
             pltpu.VMEM((8, LANES), jnp.int32),
             pltpu.VMEM((others, 8, LANES), jnp.int32),
+            dma((3,)),
             dma((3,)),
             dma((2,)),
             dma((2,)),
@@ -242,48 +252,62 @@
             dma((slabs - 1,)),
         ],
         compiler_params=pltpu.CompilerParams(
-            collective_id=0, has_side_effects=True, vmem_limit_bytes=24 * 1024 * 1024
+            collective_id=0, has_side_effects=True, vmem_limit_bytes=16 * 1024 * 1024
         ),
         cost_estimate=pl.CostEstimate(
-            flops=4 * slots * padded * half, bytes_accessed=60_000_000, transcendentals=0
+            flops=4 * slots * tokens * half, bytes_accessed=60_000_000, transcendentals=0
         ),
         name="route_rows",
-    )(ids, out_grad)
-
-
-def adam_kernel(ids_ref, got_ref, table_ref, m1_ref, m2_ref, t_out, m1_out, m2_out, onehot_ref):
-    slab_rows = table_ref.shape[0]
-
-    @pl.when(pl.program_id(0) == 0)
-    def _():
-        first = lax.axis_index("vocab") * slab_rows
-        row = lax.broadcasted_iota(jnp.int32, onehot_ref.shape, 0) + first
-        onehot_ref[...] = (
-            (row == ids_ref[0:1, :]).astype(jnp.float32).astype(jnp.bfloat16)
-        )
-
-    grad = jnp.dot(onehot_ref[...], got_ref[...], preferred_element_type=jnp.float32)
-    t_out[...], m1_out[...], m2_out[...] = adam(grad, table_ref[...], m1_ref[...], m2_ref[...])
+    )(ids, out_grad, table, moment1, moment2)
+
+
+def adam_kernel(
+    ids_ref, got_ref, table_ref, m1_ref, m2_ref, t_out, m1_out, m2_out, onehot_ref, new_ref, sem
+):
+    slab_rows, half = table_ref.shape
+    step = min(half, 256)
+    first = lax.axis_index("vocab") * slab_rows
+    row = lax.broadcasted_iota(jnp.int32, onehot_ref.shape, 0) + first
+    onehot_ref[...] = (row == ids_ref[0:1, :]).astype(jnp.float32).astype(jnp.bfloat16)
+
+    def copies(c):
+        at = pl.ds(pl.multiple_of(c * step, step), step)
+        return [
+            pltpu.make_async_copy(new_ref.at[i, :, at], out.at[:, at], sem.at[i, c])
+            for i, out in enumerate((t_out, m1_out, m2_out))
+        ]
+
+    @pl.loop(0, half // step)
+    def _(c):
+        at = pl.ds(pl.multiple_of(c * step, step), step)
+        grad = jnp.dot(onehot_ref[...], got_ref[:, at], preferred_element_type=jnp.float32)
+        new_values = adam(grad, table_ref[:, at], m1_ref[:, at], m2_ref[:, at])
+        for i, value in enumerate(new_values):
+            new_ref[i, :, at] = value
+        for copy in copies(c):
+            copy.start()
+
+    @pl.loop(0, half // step)
+    def _(c):
+        for copy in copies(c):
+            copy.wait()
 
 
 def update(got, got_ids, table, moment1, moment2):
     slab_rows, half = table.shape
     slots = got.shape[0]
-    step = min(half, 256)
-    tile = pl.BlockSpec((slab_rows, step), lambda c: (0, c))
     shape = jax.ShapeDtypeStruct(table.shape, jnp.float32)
     return pl.pallas_call(
         adam_kernel,
-        grid=(half // step,),
         out_shape=(shape,) * 3,
-        in_specs=[
-            pl.BlockSpec((8, slots), lambda c: (0, 0)),
-            pl.BlockSpec((slots, step), lambda c: (0, c)),
-            tile, tile, tile,
+        in_specs=[pl.BlockSpec(memory_space=pltpu.VMEM)] * 5,
+        out_specs=(pl.BlockSpec(memory_space=pl.ANY),) * 3,
+        scratch_shapes=[
+            pltpu.VMEM((slab_rows, slots), jnp.bfloat16),
+            pltpu.VMEM((3, slab_rows, half), jnp.float32),
+            pltpu.SemaphoreType.DMA((3, half // min(half, 256))),
         ],
-        out_specs=(tile,) * 3,
-        scratch_shapes=[pltpu.VMEM((slab_rows, slots), jnp.bfloat16)],
-        compiler_params=pltpu.CompilerParams(vmem_limit_bytes=16 * 1024 * 1024),
+        compiler_params=pltpu.CompilerParams(vmem_limit_bytes=30 * 1024 * 1024),
         cost_estimate=pl.CostEstimate(
             flops=2 * slab_rows * slots * half,
             bytes_accessed=24 * slab_rows * half,
@@ -294,8 +318,8 @@
 
 
 def per_device(groups, slabs, out_grad, token_ids, table, moment1, moment2):
-    got, got_ids, most = route(out_grad, token_ids, groups, slabs, table.shape[0])
-    outs = update(got, got_ids, table, moment1, moment2)
+    got, got_ids, most, *near = route(out_grad, token_ids, table, moment1, moment2, groups, slabs)
+    outs = update(got, got_ids, *near)
 
     def again(carry):
         return (jnp.int32(0),) + dense_update(out_grad, token_ids, table, moment1, moment2)

time: 74.5 us -> 68 us (0.913)
  Pallas kernels: 58.4 us -> 52.7 us
    pallas_call x2, Pallas kernels: 58.4 us -> 52.7 us  [the longest x1 47.1 us: route(): pl.pallas_call(functools.partial(route_kernel, groups, slabs, table.shape...]
where the time goes in v2:
time: 68 us; the launch traced here: 67.8 us
  Pallas kernels  52.7 us (78%)
  between operations  14 us (21%)
    pallas_call x1, Pallas kernels, route(): pl.pallas_call(functools.partial(route_kernel, groups, slabs, table.shape...  47.1 us
    pallas_call x1, Pallas kernels, update(): pl.pallas_call(adam_kernel, out_shape=(shape,) * 3, in_specs=[pl.BlockSpe...  5.66 us

profile of v2, /device:TPU:0, one launch (start us, length us, event | category | flops | bytes accessed | tf_op | source)
XLA Modules:
  0.0 67.8 jit_solution(11798522452006344497)
XLA Ops:
  7.2 47.1 %route_rows.1 = (bf16[384,2048]{1,0:T(8,128)(2,1)S(1)}, s32[8,384]{1,0:T(8,128)S(1)}, s32[8,128]{1,0:T(8,128)S(1)}, f32[448,2048]{1,0:T(8,128)S(1)}, f32[448,2048]{1,0:T(8,128)S(1)}, /*index=5*/f32[448,2048]{1,0:T(8,128)S(1)}) custom-call(s32[1,192]{1,0:T(1,128)} %bitcast.4, bf16[192,4096]{1,0:T(8,128)(2,1)} %grad_ref.1, f32[448,2048]{1,0:T(8,128)} %table_ref.1, ...), custom_call_target="tpu_custom_call" | custom-call | flops 603979776 | bytes 60000000 | tf_op jit(solution)/shard_map/route_rows/pallas_call | solution.py:226
  54.2 0.5 slice.3
  54.7 0.0 copy-start
  54.7 5.7 %adam_update.1 = (f32[448,2048]{1,0:T(8,128)}, f32[448,2048]{1,0:T(8,128)}, f32[448,2048]{1,0:T(8,128)}) custom-call(s32[8,384]{1,0:T(8,128)S(1)} %get-tuple-element.58.ids_ref, bf16[384,2048]{1,0:T(8,128)(2,1)S(1)} %get-tuple-element.59.got_ref, f32[448,2048]{1,0:T(8,128)S(1)} %get-tuple-element.60.table_ref, f32[448,2048]{1,0:T(8,128)S(1)} %get-tuple-element.61.m1_ref, ...), custom_call_target="tpu_custom_call" | custom-call | flops 704643072 | bytes 22020096 | tf_op jit(solution)/shard_map/adam_update/pallas_call | solution.py:300
  60.4 0.0 copy-done
  60.4 0.6 while.13
Async XLA Ops:
  54.7 5.7 %copy-start = (s32[192]{0:T(256)S(1)}, s32[192]{0:T(256)}, u32[]{:S(2)}) copy-start(s32[192]{0:T(256)} %param.8) | copy-start | bytes 2308

commit v3 on v2

--- a/solution.py
+++ b/solution.py
@@ -9,6 +9,9 @@
 
 STEP = 10
 BLOCK_ROWS = 48
+FAR_ROWS = 32
+SPILL_ROWS = BLOCK_ROWS - FAR_ROWS
+CHUNKS = 2
 LANES = 128
 FIRST_FIX = 1.0 - 0.9**STEP
 SECOND_FIX = 1.0 - 0.999**STEP
@@ -37,7 +40,7 @@
     return adam(grad, table, moment1, moment2)
 
 
-def find_slots(ids, slabs, slab_rows):
+def find_slots(ids, me, slabs, slab_rows):
     tokens = ids.shape[1]
     row = lax.broadcasted_iota(jnp.int32, (tokens, tokens), 0)
     lane = lax.broadcasted_iota(jnp.int32, (tokens, tokens), 1)
@@ -57,19 +60,36 @@
         preferred_element_type=jnp.float32,
     )
     rank = jnp.sum(member * ahead, axis=0, keepdims=True)
-    most = jnp.max(first * (rank + 1.0), axis=1, keepdims=True)
-    fits = jnp.where(rank < float(BLOCK_ROWS), first, 0.0)
-    slot_first = fits * (slab * float(BLOCK_ROWS) + rank + 1.0) - 1.0
+    split = lax.convert_element_type(me // (slabs // 2), jnp.float32)
+    partner = lax.convert_element_type(lax.rem(me + slabs // 2, slabs), jnp.float32)
+    far = jnp.where(jnp.where(slab >= float(slabs // 2), 1.0, 0.0) == split, 0.0, 1.0)
+    direct = jnp.where(rank < float(BLOCK_ROWS) - far * float(SPILL_ROWS), first, 0.0)
+    spilled = (first - direct) * far
+    spill_rank = jnp.dot(
+        jnp.broadcast_to(spilled, (8, tokens)).astype(jnp.bfloat16), before.astype(jnp.bfloat16),
+        preferred_element_type=jnp.float32,
+    )[0:1]
+    spilled = jnp.where(spill_rank < float(SPILL_ROWS), spilled, 0.0)
+    fits = direct + spilled
+    lost = jnp.max(first - fits, axis=1, keepdims=True)
+    region = direct * slab + spilled * partner
+    offset = direct * rank + spilled * (float(FAR_ROWS) + spill_rank)
+    slot_first = fits * (region * float(BLOCK_ROWS) + offset + 1.0) - 1.0
 
     field = lax.broadcasted_iota(jnp.int32, (8, tokens), 0)
     facts = jnp.where(
-        field == 0, fits * slab, jnp.where(field == 1, fits * rank, jnp.where(field == 2, fits, 0.0))
+        field == 0, region, jnp.where(field == 1, offset, jnp.where(field == 2, fits, 0.0))
     )
     facts = jnp.dot(
         facts.astype(jnp.bfloat16), same.astype(jnp.bfloat16), preferred_element_type=jnp.float32
     )
     slot = facts[0:1] * float(BLOCK_ROWS) + facts[1:2] + facts[2:3] - 1.0
-    return slot, slot_first, ids_down, most
+    return slot, slot_first, ids_down, lost
+
+
+def paired(me, d, count):
+    bits = [lax.rem(me // (1 << k), 2) for k in range(count.bit_length() - 1)]
+    return sum((1 - bit if d >> k & 1 else bit) * (1 << k) for k, bit in enumerate(bits))
 
 
 def route_kernel(
@@ -78,7 +98,7 @@
     got_ref, got_ids_ref, most_ref, near_table, near_m1, near_m2,
     rows_ref, other_ids_ref, send_ref, note_ref, got_note_ref, count_ref, got_count_ref,
     local_sem, near_sem, pair_send, pair_recv, count_send, count_recv,
-    note_send, note_recv, block_send, block_recv,
+    note_send, note_recv, block_send, block_recv, spill_send, spill_recv,
 ):
     tokens, width = grad_ref.shape
     half = width // 2
@@ -86,7 +106,9 @@
     group, me, core = lax.axis_index("groups"), lax.axis_index("vocab"), lax.axis_index("seq")
     sibling = (group, me, 1 - core)
     twins = [(lax.rem(group + d, groups), me, core) for d in range(1, groups)]
-    peers = [lax.rem(me + d, slabs) for d in range(1, slabs)]
+    across = slabs // 2
+    steps = [across] + list(range(across + 1, slabs)) + list(range(1, across))
+    peers = [paired(me, d, slabs) for d in steps]
 
     barrier = pltpu.get_barrier_semaphore()
     for device in [sibling] + twins + [(group, peer, core) for peer in peers]:
@@ -121,7 +143,7 @@
     ids = jnp.concatenate(
         [jnp.where(core == 0, mine, other), jnp.where(core == 0, other, mine)], axis=1
     ).astype(jnp.float32)
-    slot, slot_first, ids_down, most = find_slots(ids, slabs, slab_rows)
+    slot, slot_first, ids_down, most = find_slots(ids, me, slabs, slab_rows)
 
     count_ref[...] = jnp.broadcast_to(most.astype(jnp.int32), count_ref.shape)
     count_copies = []
@@ -138,26 +160,26 @@
     ).astype(jnp.float32).astype(jnp.bfloat16)
     own_rows.wait()
     rows_copy.wait()
-    step = min(half, 512)
-
-    @pl.loop(0, half // step)
-    def _(c):
-        at = pl.ds(pl.multiple_of(c * step, step), step)
+    step = half // CHUNKS
+
+    def block(k, start=0, rows=BLOCK_ROWS):
+        return pl.ds(pl.multiple_of(k * BLOCK_ROWS + start, 16), rows)
+
+    block_copies = []
+    for c in range(CHUNKS):
+        at = slice(c * step, (c + 1) * step)
         send_ref[:, at] = jnp.dot(
             gather, rows_ref[:, at], preferred_element_type=jnp.float32
         ).astype(jnp.bfloat16)
-
-    def block(k):
-        return pl.ds(pl.multiple_of(k * BLOCK_ROWS, BLOCK_ROWS), BLOCK_ROWS)
-
-    block_copies = []
-    for d, peer in enumerate(peers):
-        copy = pltpu.make_async_remote_copy(
-            send_ref.at[block(peer)], got_ref.at[block(me)], block_send.at[d], block_recv.at[d],
-            device_id=(group, peer, core), device_id_type=MESH,
-        )
-        copy.start()
-        block_copies.append(copy)
+        for d, peer in enumerate(peers):
+            rows = FAR_ROWS if steps[d] > across else BLOCK_ROWS
+            copy = pltpu.make_async_remote_copy(
+                send_ref.at[block(peer, 0, rows), at], got_ref.at[block(me, 0, rows), at],
+                block_send.at[c, d], block_recv.at[c, d],
+                device_id=(group, peer, core), device_id_type=MESH,
+            )
+            copy.start()
+            block_copies.append(copy)
     own_block = pltpu.make_async_copy(
         send_ref.at[block(me)], got_ref.at[block(me)], local_sem.at[1]
     )
@@ -175,7 +197,8 @@
     sub = lax.broadcasted_iota(jnp.int32, (8, LANES), 0)
     slot_down = slot_down.astype(jnp.int32)
     for k in range(slabs):
-        chosen = (slot_down == lane + k * BLOCK_ROWS) & (lane < BLOCK_ROWS)
+        region = jnp.where((k // across != me // across) & (lane >= FAR_ROWS), peers[0], k)
+        chosen = (slot_down == lane + region * BLOCK_ROWS) & (lane < BLOCK_ROWS)
         note = jnp.sum(jnp.where(chosen, ids_down + 1.0, 0.0), axis=0, keepdims=True) - 1.0
         note_ref[k] = jnp.where(sub == 0, note, most).astype(jnp.int32)
     note_copies = []
@@ -189,6 +212,20 @@
     own_note = pltpu.make_async_copy(note_ref.at[me], got_note_ref.at[me], local_sem.at[2])
     own_note.start()
     own_note.wait()
+
+    spill_copies = []
+    for c in range(CHUNKS):
+        at = slice(c * step, (c + 1) * step)
+        block_copies[c * len(peers)].wait()
+        shared = block(peers[0], FAR_ROWS, SPILL_ROWS)
+        for d in range(1, across):
+            copy = pltpu.make_async_remote_copy(
+                got_ref.at[shared, at], got_ref.at[shared, at],
+                spill_send.at[c, d - 1], spill_recv.at[c, d - 1],
+                device_id=(group, paired(me, d, slabs), core), device_id_type=MESH,
+            )
+            copy.start()
+            spill_copies.append(copy)
     for copy in note_copies:
         copy.wait()
 
@@ -210,7 +247,10 @@
     for copy in near:
         copy.wait()
     own_block.wait()
-    for copy in block_copies:
+    for at, copy in enumerate(block_copies):
+        if at % len(peers):
+            copy.wait()
+    for copy in spill_copies:
         copy.wait()
 
 
@@ -248,8 +288,10 @@
             dma((others,)),
             dma((slabs - 1,)),
             dma((slabs - 1,)),
-            dma((slabs - 1,)),
-            dma((slabs - 1,)),
+            dma((CHUNKS, slabs - 1)),
+            dma((CHUNKS, slabs - 1)),
+            dma((CHUNKS, slabs // 2 - 1)),
+            dma((CHUNKS, slabs // 2 - 1)),
         ],
         compiler_params=pltpu.CompilerParams(
             collective_id=0, has_side_effects=True, vmem_limit_bytes=16 * 1024 * 1024
@@ -324,7 +366,7 @@
     def again(carry):
         return (jnp.int32(0),) + dense_update(out_grad, token_ids, table, moment1, moment2)
 
-    return lax.while_loop(lambda carry: carry[0] > BLOCK_ROWS, again, (most[0, 0],) + tuple(outs))[1:]
+    return lax.while_loop(lambda carry: carry[0] > 0, again, (most[0, 0],) + tuple(outs))[1:]
 
 
 def solution(mesh):

time: 68 us -> 58.9 us (0.87)
  Pallas kernels: 52.7 us -> 43.6 us
    pallas_call x1, Pallas kernels: 47.1 us -> 38 us  [route(): pl.pallas_call(functools.partial(route_kernel, groups, slabs, table.shape...]
where the time goes in v3:
time: 58.9 us; the launch traced here: 58.7 us
  Pallas kernels  43.6 us (74%)
  between operations  14 us (24%)
    pallas_call x1, Pallas kernels, route(): pl.pallas_call(functools.partial(route_kernel, groups, slabs, table.shape...  38 us
    pallas_call x1, Pallas kernels, update(): pl.pallas_call(adam_kernel, out_shape=(shape,) * 3, in_specs=[pl.BlockSpe...  5.65 us

profile of v3, /device:TPU:0, one launch (start us, length us, event | category | flops | bytes accessed | tf_op | source)
XLA Modules:
  0.0 58.7 jit_solution(3390008675580289876)
XLA Ops:
  7.2 38.0 %route_rows.1 = (bf16[384,2048]{1,0:T(8,128)(2,1)S(1)}, s32[8,384]{1,0:T(8,128)S(1)}, s32[8,128]{1,0:T(8,128)S(1)}, f32[448,2048]{1,0:T(8,128)S(1)}, f32[448,2048]{1,0:T(8,128)S(1)}, /*index=5*/f32[448,2048]{1,0:T(8,128)S(1)}) custom-call(s32[1,192]{1,0:T(1,128)} %bitcast.4, bf16[192,4096]{1,0:T(8,128)(2,1)} %grad_ref.1, f32[448,2048]{1,0:T(8,128)} %table_ref.1, ...), custom_call_target="tpu_custom_call" | custom-call | flops 603979776 | bytes 60000000 | tf_op jit(solution)/shard_map/route_rows/pallas_call | solution.py:266
  45.1 0.5 slice.3
  45.6 0.0 copy-start
  45.6 5.7 %adam_update.1 = (f32[448,2048]{1,0:T(8,128)}, f32[448,2048]{1,0:T(8,128)}, f32[448,2048]{1,0:T(8,128)}) custom-call(s32[8,384]{1,0:T(8,128)S(1)} %get-tuple-element.58.ids_ref, bf16[384,2048]{1,0:T(8,128)(2,1)S(1)} %get-tuple-element.59.got_ref, f32[448,2048]{1,0:T(8,128)S(1)} %get-tuple-element.60.table_ref, f32[448,2048]{1,0:T(8,128)S(1)} %get-tuple-element.61.m1_ref, ...), custom_call_target="tpu_custom_call" | custom-call | flops 704643072 | bytes 22020096 | tf_op jit(solution)/shard_map/adam_update/pallas_call | solution.py:342
  51.3 0.0 copy-done
  51.3 0.6 while.13
Async XLA Ops:
  45.6 5.7 %copy-start = (s32[192]{0:T(256)S(1)}, s32[192]{0:T(256)}, u32[]{:S(2)}) copy-start(s32[192]{0:T(256)} %param.8) | copy-start | bytes 2308

commit v4 on v3

--- a/solution.py
+++ b/solution.py
@@ -110,15 +110,18 @@
     steps = [across] + list(range(across + 1, slabs)) + list(range(1, across))
     peers = [paired(me, d, slabs) for d in steps]
 
+    def columns(which):
+        return pl.ds(pl.multiple_of(which * half, half), half)
+
+    place = pl.ds(pl.multiple_of(core * tokens, tokens), tokens)
+    own_rows = pltpu.make_async_copy(grad_ref.at[:, columns(core)], rows_ref.at[place], local_sem.at[0])
+    own_rows.start()
+
     barrier = pltpu.get_barrier_semaphore()
     for device in [sibling] + twins + [(group, peer, core) for peer in peers]:
         pl.semaphore_signal(barrier, inc=1, device_id=device, device_id_type=MESH)
     pl.semaphore_wait(barrier, groups + slabs - 1)
 
-    def columns(which):
-        return pl.ds(pl.multiple_of(which * half, half), half)
-
-    place = pl.ds(pl.multiple_of(core * tokens, tokens), tokens)
     ids_copy = pltpu.make_async_remote_copy(
         ids_ref, other_ids_ref, pair_send.at[0], pair_recv.at[0],
         device_id=sibling, device_id_type=MESH,
@@ -129,8 +132,6 @@
         device_id=sibling, device_id_type=MESH,
     )
     rows_copy.start()
-    own_rows = pltpu.make_async_copy(grad_ref.at[:, columns(core)], rows_ref.at[place], local_sem.at[0])
-    own_rows.start()
     near = [
         pltpu.make_async_copy(far_ref, near_ref, near_sem.at[i])
         for i, (far_ref, near_ref) in enumerate(
@@ -165,21 +166,29 @@
     def block(k, start=0, rows=BLOCK_ROWS):
         return pl.ds(pl.multiple_of(k * BLOCK_ROWS + start, 16), rows)
 
-    block_copies = []
+    block_copies = {}
+
+    def send(c, d):
+        at = slice(c * step, (c + 1) * step)
+        rows = FAR_ROWS if steps[d] > across else BLOCK_ROWS
+        copy = pltpu.make_async_remote_copy(
+            send_ref.at[block(peers[d], 0, rows), at], got_ref.at[block(me, 0, rows), at],
+            block_send.at[c, d], block_recv.at[c, d],
+            device_id=(group, peers[d], core), device_id_type=MESH,
+        )
+        copy.start()
+        block_copies[c, d] = copy
+
     for c in range(CHUNKS):
         at = slice(c * step, (c + 1) * step)
         send_ref[:, at] = jnp.dot(
             gather, rows_ref[:, at], preferred_element_type=jnp.float32
         ).astype(jnp.bfloat16)
-        for d, peer in enumerate(peers):
-            rows = FAR_ROWS if steps[d] > across else BLOCK_ROWS
-            copy = pltpu.make_async_remote_copy(
-                send_ref.at[block(peer, 0, rows), at], got_ref.at[block(me, 0, rows), at],
-                block_send.at[c, d], block_recv.at[c, d],
-                device_id=(group, peer, core), device_id_type=MESH,
-            )
-            copy.start()
-            block_copies.append(copy)
+        for d in range(slabs - across):
+            send(c, d)
+    for c in range(CHUNKS):
+        for d in range(slabs - across, len(peers)):
+            send(c, d)
     own_block = pltpu.make_async_copy(
         send_ref.at[block(me)], got_ref.at[block(me)], local_sem.at[1]
     )
@@ -216,7 +225,7 @@
     spill_copies = []
     for c in range(CHUNKS):
         at = slice(c * step, (c + 1) * step)
-        block_copies[c * len(peers)].wait()
+        block_copies[c, 0].wait()
         shared = block(peers[0], FAR_ROWS, SPILL_ROWS)
         for d in range(1, across):
             copy = pltpu.make_async_remote_copy(
@@ -247,8 +256,8 @@
     for copy in near:
         copy.wait()
     own_block.wait()
-    for at, copy in enumerate(block_copies):
-        if at % len(peers):
+    for (_, d), copy in block_copies.items():
+        if d:
             copy.wait()
     for copy in spill_copies:
         copy.wait()
@@ -307,7 +316,7 @@
     ids_ref, got_ref, table_ref, m1_ref, m2_ref, t_out, m1_out, m2_out, onehot_ref, new_ref, sem
 ):
     slab_rows, half = table_ref.shape
-    step = min(half, 256)
+    step = min(half, 512)
     first = lax.axis_index("vocab") * slab_rows
     row = lax.broadcasted_iota(jnp.int32, onehot_ref.shape, 0) + first
     onehot_ref[...] = (row == ids_ref[0:1, :]).astype(jnp.float32).astype(jnp.bfloat16)
@@ -347,7 +356,7 @@
         scratch_shapes=[
             pltpu.VMEM((slab_rows, slots), jnp.bfloat16),
             pltpu.VMEM((3, slab_rows, half), jnp.float32),
-            pltpu.SemaphoreType.DMA((3, half // min(half, 256))),
+            pltpu.SemaphoreType.DMA((3, half // min(half, 512))),
         ],
         compiler_params=pltpu.CompilerParams(vmem_limit_bytes=30 * 1024 * 1024),
         cost_estimate=pl.CostEstimate(

time: 58.9 us -> 58.9 us (level)
  no operation moved by 1% of the time
where the time goes in v4:
time: 58.9 us; the launch traced here: 58.7 us
  Pallas kernels  43.6 us (74%)
  between operations  14 us (24%)
    pallas_call x1, Pallas kernels, route(): pl.pallas_call(functools.partial(route_kernel, groups, slabs, table.shape...  38.3 us
    pallas_call x1, Pallas kernels, update(): pl.pallas_call(adam_kernel, out_shape=(shape,) * 3, in_specs=[pl.BlockSpe...  5.31 us

profile of v4, /device:TPU:0, one launch (start us, length us, event | category | flops | bytes accessed | tf_op | source)
XLA Modules:
  0.0 58.7 jit_solution(11575964603669185405)
XLA Ops:
  7.2 38.3 %route_rows.1 = (bf16[384,2048]{1,0:T(8,128)(2,1)S(1)}, s32[8,384]{1,0:T(8,128)S(1)}, s32[8,128]{1,0:T(8,128)S(1)}, f32[448,2048]{1,0:T(8,128)S(1)}, f32[448,2048]{1,0:T(8,128)S(1)}, /*index=5*/f32[448,2048]{1,0:T(8,128)S(1)}) custom-call(s32[1,192]{1,0:T(1,128)} %bitcast.4, bf16[192,4096]{1,0:T(8,128)(2,1)} %grad_ref.1, f32[448,2048]{1,0:T(8,128)} %table_ref.1, ...), custom_call_target="tpu_custom_call" | custom-call | flops 603979776 | bytes 60000000 | tf_op jit(solution)/shard_map/route_rows/pallas_call | solution.py:275
  45.5 0.5 slice.3
  45.9 0.0 copy-start
  45.9 5.3 %adam_update.1 = (f32[448,2048]{1,0:T(8,128)}, f32[448,2048]{1,0:T(8,128)}, f32[448,2048]{1,0:T(8,128)}) custom-call(s32[8,384]{1,0:T(8,128)S(1)} %get-tuple-element.58.ids_ref, bf16[384,2048]{1,0:T(8,128)(2,1)S(1)} %get-tuple-element.59.got_ref, f32[448,2048]{1,0:T(8,128)S(1)} %get-tuple-element.60.table_ref, f32[448,2048]{1,0:T(8,128)S(1)} %get-tuple-element.61.m1_ref, ...), custom_call_target="tpu_custom_call" | custom-call | flops 704643072 | bytes 22020096 | tf_op jit(solution)/shard_map/adam_update/pallas_call | solution.py:351
  51.3 0.0 copy-done
  51.3 0.6 while.13
Async XLA Ops:
  45.9 5.3 %copy-start = (s32[192]{0:T(256)S(1)}, s32[192]{0:T(256)}, u32[]{:S(2)}) copy-start(s32[192]{0:T(256)} %param.8) | copy-start | bytes 2308
